TPU v7x, 512 devices: a whole 4x4x16 slice. The times are simulated.
512 devices in a mesh: blk: 256 (over z, y_lo, x, core), rep: 2 (over y_hi).
Axes of the slice: x: 4, y: 4 (y_hi: 2, y_lo: 2; y = y_hi * 2 + y_lo), z: 16, core: 2. Of those that a mesh axis runs over, the one named last changes fastest.
Arguments:
- residue_string_vectors: float32 [65536, 1024], P(('blk', 'rep')), may hold values from -0.1875 to 0.1875
- fold_shape_vectors: float32 [65536, 1024], P('blk'), may hold values from -0.1875 to 0.1875
- family_label: int32 [65536], P('blk'), may hold values from 0 to 2047, as said below
- sharpness_multiplier: float32 [1], replicated, may hold values from 4 to 12
- additive_offset_term: float32 [1], replicated, may hold values from -5 to -2
Outputs:
- loss_rows: float32 [65536], P(('blk', 'rep'))
- sequence_gradient: float32 [65536, 1024], P(('blk', 'rep'))
- structure_gradient: float32 [65536, 1024], P('blk')
Inputs may be any that keep to these rules, and one draw needn't show every extreme that they name: `family_label`: members of one cluster lie in blocks at most 8 apart along the loop of 256 blocks.
All inputs are finite; a program needn't handle non-finite values.
Results may differ from a plain program's by a relative error of at most 0.0003.
Values sent between devices are 32-bit elements; how exact they have to be, the bound alone decides.
A program may use at most 64 MiB of HBM per device.

v0:
```python
import jax
import jax.numpy as jnp
from jax import lax
from jax.sharding import PartitionSpec as P

HOPS = 4


EPSILON = 1e-06


def passed_along(x, axis, by):
    length = lax.axis_size(axis)
    return lax.ppermute(x, axis, [(i, (i + by) % length) for i in range(length)])


def unit_rows(embedding):
    length = jnp.sqrt(jnp.sum(embedding * embedding, axis=1, keepdims=True) + EPSILON)
    return (embedding / length, length)


def project_tangent(direction, unit, length):
    along = jnp.sum(unit * direction, axis=1, keepdims=True)
    return (direction - unit * along) / length


def pairwise_tile(
    residue_string_entries,
    residue_string_position,
    fold_shape_entries,
    fold_shape_position,
    sharpness_multiplier,
    additive_offset_term,
):
    angular_similarity_grid = lax.dot_general(
        residue_string_entries,
        fold_shape_entries,
        (((1,), (1,)), ((), ())),
        precision=lax.Precision.HIGHEST,
        preferred_element_type=jnp.float32,
    )
    score_grid = sharpness_multiplier[0] * angular_similarity_grid + additive_offset_term[0]
    agreement = (
        2.0 * (residue_string_position[:, None] == fold_shape_position[None, :]).astype(jnp.float32)
        - 1.0
    )
    margin = -agreement * score_grid
    loss_part = jnp.sum(jax.nn.softplus(margin), axis=1)
    weight = -agreement * jax.nn.sigmoid(margin)
    seq_part = jnp.dot(
        weight,
        fold_shape_entries,
        precision=lax.Precision.HIGHEST,
        preferred_element_type=jnp.float32,
    )
    struct_part = lax.dot_general(
        weight,
        residue_string_entries,
        (((0,), (0,)), ((), ())),
        precision=lax.Precision.HIGHEST,
        preferred_element_type=jnp.float32,
    )
    return (loss_part, seq_part, struct_part)


def finish_struct(summed, distance):
    summed = passed_along(summed, "blk", distance)
    return lax.psum(summed, "rep")


def body(
    residue_string_vectors,
    fold_shape_vectors,
    family_label,
    sharpness_multiplier,
    additive_offset_term,
):
    residue_string_unitized, residue_string_length = unit_rows(residue_string_vectors)
    fold_shape_unitized, fold_shape_length = unit_rows(fold_shape_vectors)
    seq_count = residue_string_vectors.shape[0]
    block_size = fold_shape_vectors.shape[0]
    fold_shape_position = family_label.astype(jnp.float32)
    residue_string_position = lax.dynamic_slice_in_dim(
        fold_shape_position, lax.axis_index("rep") * seq_count, seq_count
    )
    sequence_visitor, sequence_visitor_index = (residue_string_unitized, residue_string_position)
    structure_visitor, structure_visitor_index = (fold_shape_unitized, fold_shape_position)
    loss_sum = jnp.zeros((seq_count,), jnp.float32)
    residue_string_accumulated = jnp.zeros_like(residue_string_unitized)
    fold_shape_accumulated = jnp.zeros_like(fold_shape_unitized)
    for stride in range(HOPS + 1):
        if stride > 0:
            sequence_visitor, sequence_visitor_index = passed_along(
                (sequence_visitor, sequence_visitor_index), "blk", 1
            )
            structure_visitor, structure_visitor_index = passed_along(
                (structure_visitor, structure_visitor_index), "blk", -1
            )
        loss_part, seq_part, struct_part = pairwise_tile(
            sequence_visitor,
            sequence_visitor_index,
            structure_visitor,
            structure_visitor_index,
            sharpness_multiplier,
            additive_offset_term,
        )
        loss_sum = loss_sum + loss_part
        residue_string_accumulated = residue_string_accumulated + seq_part
        fold_shape_accumulated = fold_shape_accumulated + struct_part
        if stride < HOPS:
            loss_sum, residue_string_accumulated = passed_along(
                (loss_sum, residue_string_accumulated), "blk", 1
            )
            fold_shape_accumulated = passed_along(fold_shape_accumulated, "blk", -1)
    loss_sum, residue_string_accumulated = passed_along(
        (loss_sum, residue_string_accumulated), "blk", -HOPS
    )
    fold_shape_direction = finish_struct(fold_shape_accumulated, HOPS)
    sequence_gradient = project_tangent(
        sharpness_multiplier[0] * residue_string_accumulated,
        residue_string_unitized,
        residue_string_length,
    )
    structure_gradient = project_tangent(
        sharpness_multiplier[0] * fold_shape_direction, fold_shape_unitized, fold_shape_length
    )
    loss_rows = loss_sum / ((HOPS + 1) * block_size)
    return (loss_rows, sequence_gradient, structure_gradient)


def solution(mesh):
    placed = (P(("blk", "rep"), None), P("blk", None), P("blk"), P(), P())
    return jax.shard_map(
        body,
        mesh=mesh,
        in_specs=placed,
        out_specs=(P(("blk", "rep")), P(("blk", "rep"), None), P("blk", None)),
        check_vma=False,
    )
```

profile of v0, /device:TPU:1, one launch (start us, length us, event | category | flops | bytes accessed | tf_op | source)
XLA Modules:
  0.0 240.9 jit_solution(11278813338053568517)
XLA Ops:
  8.9 8.8 %collective-permute-start.4 = (f32[256,1024]{1,0:T(8,128)S(1)}, f32[256,1024]{1,0:T(8,128)}, u32[]{:S(2)}, u32[]{:S(2)}) collective-permute-start(f32[256,1024]{1,0:T(8,128)S(1)} %broadcast_divide_fusion), channel_id=1, source_target_pairs={{0,510},{2,0},{4,2},{6,4},{8,6},{10,8},{12,10},{14,12},{16,14},{18... | collective-permute-start | bytes 3145736 | tf_op jit(solution)/shard_map/ppermute | solution.py:14
  22.4 8.7 %collective-permute-start.26 = (f32[256,1024]{1,0:T(8,128)S(1)}, f32[256,1024]{1,0:T(8,128)S(1)}, u32[]{:S(2)}, u32[]{:S(2)}) collective-permute-start(f32[256,1024]{1,0:T(8,128)S(1)} %fusion.15), channel_id=1, source_target_pairs={{0,510},{2,0},{4,2},{6,4},{8,6},{10,8},{12,10},{14,12},{16,14},{18... | collective-permute-start | bytes 3145736 | tf_op jit(solution)/shard_map/ppermute | solution.py:14
  35.6 3.0 %collective-permute-start.1 = (f32[128]{0:T(128)S(1)}, f32[128]{0:T(128)S(1)}, u32[]{:S(2)}, u32[]{:S(2)}) collective-permute-start(f32[128]{0:T(128)S(1)} %dynamic_slice.3), channel_id=1, source_target_pairs={{0,2},{2,4},{4,6},{6,8},{8,10},{10,12},{12,14},{14,16},{16,18},{18... | collective-permute-start | bytes 1544 | tf_op jit(solution)/shard_map/ppermute | solution.py:14
  38.6 6.8 %collective-permute-start.9 = (f32[256,1024]{1,0:T(8,128)}, f32[256,1024]{1,0:T(8,128)S(1)}, u32[]{:S(2)}, u32[]{:S(2)}) collective-permute-start(f32[256,1024]{1,0:T(8,128)} %collective-permute-done.4), channel_id=1, source_target_pairs={{0,510},{2,0},{4,2},{6,4},{8,6},{10,8},{12,10},{14,12},{16,14},{18... | collective-permute-start | bytes 3145736 | tf_op jit(solution)/shard_map/ppermute | solution.py:14
  49.1 7.9 %collective-permute-start.27 = (f32[256,1024]{1,0:T(8,128)S(1)}, f32[256,1024]{1,0:T(8,128)S(1)}, u32[]{:S(2)}, u32[]{:S(2)}) collective-permute-start(f32[256,1024]{1,0:T(8,128)S(1)} %convolution_add_fusion.3), channel_id=1, source_target_pairs={{0,510},{2,0},{4,2},{6,4},{8,6},{10,8},{12,10},{14,12},{16,14},{18... | collective-permute-start | bytes 3145736 | tf_op jit(solution)/shard_map/ppermute | solution.py:14
  60.9 4.6 %collective-permute-start.7 = (f32[256]{0:T(256)S(1)}, f32[256]{0:T(256)S(1)}, u32[]{:S(2)}, u32[]{:S(2)}) collective-permute-start(f32[256]{0:T(256)S(1)} %collective-permute-done.2), channel_id=1, source_target_pairs={{0,510},{2,0},{4,2},{6,4},{8,6},{10,8},{12,10},{14,12},{16,14},{18... | collective-permute-start | bytes 3080 | tf_op jit(solution)/shard_map/ppermute | solution.py:14
  66.2 3.2 %collective-permute-start.21 = (f32[128,1024]{1,0:T(8,128)S(1)}, f32[128,1024]{1,0:T(8,128)S(1)}, u32[]{:S(2)}, u32[]{:S(2)}) collective-permute-start(f32[128,1024]{1,0:T(8,128)S(1)} %fusion.16), channel_id=1, source_target_pairs={{0,2},{2,4},{4,6},{6,8},{8,10},{10,12},{12,14},{14,16},{16,18},{18... | collective-permute-start | bytes 1572872 | tf_op jit(solution)/shard_map/ppermute | solution.py:14
  69.5 8.8 %collective-permute-start.14 = (f32[256,1024]{1,0:T(8,128)S(1)}, f32[256,1024]{1,0:T(8,128)S(1)}, u32[]{:S(2)}, u32[]{:S(2)}) collective-permute-start(f32[256,1024]{1,0:T(8,128)S(1)} %collective-permute-done.9), channel_id=1, source_target_pairs={{0,510},{2,0},{4,2},{6,4},{8,6},{10,8},{12,10},{14,12},{16,14},{18... | collective-permute-start | bytes 3145736 | tf_op jit(solution)/shard_map/ppermute | solution.py:14
  80.8 7.9 %collective-permute-start.28 = (f32[256,1024]{1,0:T(8,128)S(1)}, f32[256,1024]{1,0:T(8,128)S(1)}, u32[]{:S(2)}, u32[]{:S(2)}) collective-permute-start(f32[256,1024]{1,0:T(8,128)S(1)} %convolution_add_fusion.2), channel_id=1, source_target_pairs={{0,510},{2,0},{4,2},{6,4},{8,6},{10,8},{12,10},{14,12},{16,14},{18... | collective-permute-start | bytes 3145736 | tf_op jit(solution)/shard_map/ppermute | solution.py:14
  96.9 4.2 %collective-permute-start.22 = (f32[128,1024]{1,0:T(8,128)S(1)}, f32[128,1024]{1,0:T(8,128)S(1)}, u32[]{:S(2)}, u32[]{:S(2)}) collective-permute-start(f32[128,1024]{1,0:T(8,128)S(1)} %convolution_add_fusion.7), channel_id=1, source_target_pairs={{0,2},{2,4},{4,6},{6,8},{8,10},{10,12},{12,14},{14,16},{16,18},{18... | collective-permute-start | bytes 1572872 | tf_op jit(solution)/shard_map/ppermute | solution.py:14
  101.2 6.3 %collective-permute-start.19 = (f32[256,1024]{1,0:T(8,128)S(1)}, f32[256,1024]{1,0:T(8,128)S(1)}, u32[]{:S(2)}, u32[]{:S(2)}) collective-permute-start(f32[256,1024]{1,0:T(8,128)S(1)} %collective-permute-done.14), channel_id=1, source_target_pairs={{0,510},{2,0},{4,2},{6,4},{8,6},{10,8},{12,10},{14,12},{16,14},{18... | collective-permute-start | bytes 3145736 | tf_op jit(solution)/shard_map/ppermute | solution.py:14
  110.0 7.9 %collective-permute-start.29 = (f32[256,1024]{1,0:T(8,128)S(1)}, f32[256,1024]{1,0:T(8,128)S(1)}, u32[]{:S(2)}, u32[]{:S(2)}) collective-permute-start(f32[256,1024]{1,0:T(8,128)S(1)} %convolution_add_fusion.1), channel_id=1, source_target_pairs={{0,510},{2,0},{4,2},{6,4},{8,6},{10,8},{12,10},{14,12},{16,14},{18... | collective-permute-start | bytes 3145736 | tf_op jit(solution)/shard_map/ppermute | solution.py:14
  125.9 4.4 %collective-permute-start.23 = (f32[128,1024]{1,0:T(8,128)S(1)}, f32[128,1024]{1,0:T(8,128)S(1)}, u32[]{:S(2)}, u32[]{:S(2)}) collective-permute-start(f32[128,1024]{1,0:T(8,128)S(1)} %convolution_add_fusion.6), channel_id=1, source_target_pairs={{0,2},{2,4},{4,6},{6,8},{8,10},{10,12},{12,14},{14,16},{16,18},{18... | collective-permute-start | bytes 1572872 | tf_op jit(solution)/shard_map/ppermute | solution.py:14
  137.2 4.5 %collective-permute-start.24 = (f32[128,1024]{1,0:T(8,128)S(1)}, f32[128,1024]{1,0:T(8,128)}, u32[]{:S(2)}, u32[]{:S(2)}) collective-permute-start(f32[128,1024]{1,0:T(8,128)S(1)} %convolution_add_fusion.5), channel_id=1, source_target_pairs={{0,2},{2,4},{4,6},{6,8},{8,10},{10,12},{12,14},{14,16},{16,18},{18... | collective-permute-start | bytes 1572872 | tf_op jit(solution)/shard_map/ppermute | solution.py:14
  141.7 20.2 %collective-permute-done.30 = f32[256,1024]{1,0:T(8,128)} collective-permute-done((f32[256,1024]{1,0:T(8,128)S(1)}, f32[256,1024]{1,0:T(8,128)}, u32[]{:S(2)}, u32[]{:S(2)}) %collective-permute-start.30) | collective-permute-done | bytes 1048608 | tf_op jit(solution)/shard_map/ppermute | solution.py:14
  161.9 4.0 %collective-permute-done.24 = f32[128,1024]{1,0:T(8,128)} collective-permute-done((f32[128,1024]{1,0:T(8,128)S(1)}, f32[128,1024]{1,0:T(8,128)}, u32[]{:S(2)}, u32[]{:S(2)}) %collective-permute-start.24) | collective-permute-done | bytes 524320 | tf_op jit(solution)/shard_map/ppermute | solution.py:14
  167.7 4.3 %collective-permute-start.25 = (f32[128,1024]{1,0:T(8,128)S(1)}, f32[128,1024]{1,0:T(8,128)S(1)}, u32[]{:S(2)}, u32[]{:S(2)}) collective-permute-start(f32[128,1024]{1,0:T(8,128)S(1)} %convolution_add_fusion.4), channel_id=1, source_target_pairs={{0,504},{2,506},{4,508},{6,510},{8,0},{10,2},{12,4},{14,6},{16,8},... | collective-permute-start | bytes 1572872 | tf_op jit(solution)/shard_map/ppermute | solution.py:14
  171.9 7.8 %collective-permute-start = (f32[128]{0:T(128)S(1)}, f32[128]{0:T(128)S(1)}, u32[]{:S(2)}, u32[]{:S(2)}) collective-permute-start(f32[128]{0:T(128)S(1)} %get-tuple-element.3), channel_id=1, source_target_pairs={{0,2},{2,4},{4,6},{6,8},{8,10},{10,12},{12,14},{14,16},{16,18},{18... | collective-permute-start | bytes 1544 | tf_op jit(solution)/shard_map/ppermute | solution.py:14
  179.7 6.6 %collective-permute-done = f32[128]{0:T(128)S(1)} collective-permute-done((f32[128]{0:T(128)S(1)}, f32[128]{0:T(128)S(1)}, u32[]{:S(2)}, u32[]{:S(2)}) %collective-permute-start) | collective-permute-done | bytes 544 | tf_op jit(solution)/shard_map/ppermute | solution.py:14
  188.2 7.2 %collective-permute-done.5 = f32[128]{0:T(128)S(1)} collective-permute-done((f32[128]{0:T(128)S(1)}, f32[128]{0:T(128)S(1)}, u32[]{:S(2)}, u32[]{:S(2)}) %collective-permute-start.5) | collective-permute-done | bytes 544 | tf_op jit(solution)/shard_map/ppermute | solution.py:14
  197.3 7.2 %collective-permute-done.10 = f32[128]{0:T(128)S(1)} collective-permute-done((f32[128]{0:T(128)S(1)}, f32[128]{0:T(128)S(1)}, u32[]{:S(2)}, u32[]{:S(2)}) %collective-permute-start.10) | collective-permute-done | bytes 544 | tf_op jit(solution)/shard_map/ppermute | solution.py:14
  206.4 7.2 %collective-permute-done.15 = f32[128]{0:T(128)S(1)} collective-permute-done((f32[128]{0:T(128)S(1)}, f32[128]{0:T(128)S(1)}, u32[]{:S(2)}, u32[]{:S(2)}) %collective-permute-start.15) | collective-permute-done | bytes 544 | tf_op jit(solution)/shard_map/ppermute | solution.py:14
  215.4 3.9 %collective-permute-done.20 = f32[128]{0:T(128)S(1)} collective-permute-done((f32[128]{0:T(128)S(1)}, f32[128]{0:T(128)S(1)}, u32[]{:S(2)}, u32[]{:S(2)}) %collective-permute-start.20) | collective-permute-done | bytes 544 | tf_op jit(solution)/shard_map/ppermute | solution.py:14
  221.0 10.3 %all-reduce.2.cloned.1.call-done = f32[256,1024]{1,0:T(8,128)} async-done(((f32[256,1024]{1,0:T(8,128)}), f32[256,1024]{1,0:T(8,128)}) %all-reduce.2.cloned.1.call-update) | async-done | bytes 1048592 | tf_op jit(solution)/shard_map/psum | solution.py:68
  (85 shorter events, 59.7 us)
Async XLA Ops:
  7.2 224.1 %all-reduce.2.cloned.1.call-start = ((), (), s32[]{:S(2)}) async-start(), calls=%async_computation | async-start | bytes 2097152 | tf_op jit(solution)/shard_map/psum | solution.py:68
  8.9 29.7 %collective-permute-start.4 = (f32[256,1024]{1,0:T(8,128)S(1)}, f32[256,1024]{1,0:T(8,128)}, u32[]{:S(2)}, u32[]{:S(2)}) collective-permute-start(f32[256,1024]{1,0:T(8,128)S(1)} %broadcast_divide_fusion), channel_id=1, source_target_pairs={{0,510},{2,0},{4,2},{6,4},{8,6},{10,8},{12,10},{14,12},{16,14},{18... | collective-permute-start | bytes 3145736 | tf_op jit(solution)/shard_map/ppermute | solution.py:14
  22.4 25.6 %collective-permute-start.26 = (f32[256,1024]{1,0:T(8,128)S(1)}, f32[256,1024]{1,0:T(8,128)S(1)}, u32[]{:S(2)}, u32[]{:S(2)}) collective-permute-start(f32[256,1024]{1,0:T(8,128)S(1)} %fusion.15), channel_id=1, source_target_pairs={{0,510},{2,0},{4,2},{6,4},{8,6},{10,8},{12,10},{14,12},{16,14},{18... | collective-permute-start | bytes 3145736 | tf_op jit(solution)/shard_map/ppermute | solution.py:14
  31.1 14.3 %collective-permute-start.3 = (f32[128,1024]{1,0:T(8,128)S(1)}, f32[128,1024]{1,0:T(8,128)S(1)}, u32[]{:S(2)}, u32[]{:S(2)}) collective-permute-start(f32[128,1024]{1,0:T(8,128)S(1)} %broadcast_divide_fusion.1), channel_id=1, source_target_pairs={{0,2},{2,4},{4,6},{6,8},{8,10},{10,12},{12,14},{14,16},{16,18},{18... | collective-permute-start | bytes 1572872 | tf_op jit(solution)/shard_map/ppermute | solution.py:14
  33.0 12.4 %collective-permute-start.2 = (f32[256]{0:T(256)S(1)}, f32[256]{0:T(256)S(1)}, u32[]{:S(2)}, u32[]{:S(2)}) collective-permute-start(f32[256]{0:T(256)S(1)} %convert_element_type.2), channel_id=1, source_target_pairs={{0,510},{2,0},{4,2},{6,4},{8,6},{10,8},{12,10},{14,12},{16,14},{18... | collective-permute-start | bytes 3080 | tf_op jit(solution)/shard_map/ppermute | solution.py:14
  35.6 9.8 %collective-permute-start.1 = (f32[128]{0:T(128)S(1)}, f32[128]{0:T(128)S(1)}, u32[]{:S(2)}, u32[]{:S(2)}) collective-permute-start(f32[128]{0:T(128)S(1)} %dynamic_slice.3), channel_id=1, source_target_pairs={{0,2},{2,4},{4,6},{6,8},{8,10},{10,12},{12,14},{14,16},{16,18},{18... | collective-permute-start | bytes 1544 | tf_op jit(solution)/shard_map/ppermute | solution.py:14
  38.6 30.9 %collective-permute-start.9 = (f32[256,1024]{1,0:T(8,128)}, f32[256,1024]{1,0:T(8,128)S(1)}, u32[]{:S(2)}, u32[]{:S(2)}) collective-permute-start(f32[256,1024]{1,0:T(8,128)} %collective-permute-done.4), channel_id=1, source_target_pairs={{0,510},{2,0},{4,2},{6,4},{8,6},{10,8},{12,10},{14,12},{16,14},{18... | collective-permute-start | bytes 3145736 | tf_op jit(solution)/shard_map/ppermute | solution.py:14
  49.1 30.6 %collective-permute-start.27 = (f32[256,1024]{1,0:T(8,128)S(1)}, f32[256,1024]{1,0:T(8,128)S(1)}, u32[]{:S(2)}, u32[]{:S(2)}) collective-permute-start(f32[256,1024]{1,0:T(8,128)S(1)} %convolution_add_fusion.3), channel_id=1, source_target_pairs={{0,510},{2,0},{4,2},{6,4},{8,6},{10,8},{12,10},{14,12},{16,14},{18... | collective-permute-start | bytes 3145736 | tf_op jit(solution)/shard_map/ppermute | solution.py:14
  57.0 21.3 %collective-permute-start.8 = (f32[128,1024]{1,0:T(8,128)S(1)}, f32[128,1024]{1,0:T(8,128)S(1)}, u32[]{:S(2)}, u32[]{:S(2)}) collective-permute-start(f32[128,1024]{1,0:T(8,128)S(1)} %collective-permute-done.3), channel_id=1, source_target_pairs={{0,2},{2,4},{4,6},{6,8},{8,10},{10,12},{12,14},{14,16},{16,18},{18... | collective-permute-start | bytes 1572872 | tf_op jit(solution)/shard_map/ppermute | solution.py:14
  60.9 17.5 %collective-permute-start.7 = (f32[256]{0:T(256)S(1)}, f32[256]{0:T(256)S(1)}, u32[]{:S(2)}, u32[]{:S(2)}) collective-permute-start(f32[256]{0:T(256)S(1)} %collective-permute-done.2), channel_id=1, source_target_pairs={{0,510},{2,0},{4,2},{6,4},{8,6},{10,8},{12,10},{14,12},{16,14},{18... | collective-permute-start | bytes 3080 | tf_op jit(solution)/shard_map/ppermute | solution.py:14
  66.2 26.3 %collective-permute-start.21 = (f32[128,1024]{1,0:T(8,128)S(1)}, f32[128,1024]{1,0:T(8,128)S(1)}, u32[]{:S(2)}, u32[]{:S(2)}) collective-permute-start(f32[128,1024]{1,0:T(8,128)S(1)} %fusion.16), channel_id=1, source_target_pairs={{0,2},{2,4},{4,6},{6,8},{8,10},{10,12},{12,14},{14,16},{16,18},{18... | collective-permute-start | bytes 1572872 | tf_op jit(solution)/shard_map/ppermute | solution.py:14
  69.5 31.7 %collective-permute-start.14 = (f32[256,1024]{1,0:T(8,128)S(1)}, f32[256,1024]{1,0:T(8,128)S(1)}, u32[]{:S(2)}, u32[]{:S(2)}) collective-permute-start(f32[256,1024]{1,0:T(8,128)S(1)} %collective-permute-done.9), channel_id=1, source_target_pairs={{0,510},{2,0},{4,2},{6,4},{8,6},{10,8},{12,10},{14,12},{16,14},{18... | collective-permute-start | bytes 3145736 | tf_op jit(solution)/shard_map/ppermute | solution.py:14
  80.8 28.0 %collective-permute-start.28 = (f32[256,1024]{1,0:T(8,128)S(1)}, f32[256,1024]{1,0:T(8,128)S(1)}, u32[]{:S(2)}, u32[]{:S(2)}) collective-permute-start(f32[256,1024]{1,0:T(8,128)S(1)} %convolution_add_fusion.2), channel_id=1, source_target_pairs={{0,510},{2,0},{4,2},{6,4},{8,6},{10,8},{12,10},{14,12},{16,14},{18... | collective-permute-start | bytes 3145736 | tf_op jit(solution)/shard_map/ppermute | solution.py:14
  88.7 18.8 %collective-permute-start.13 = (f32[128,1024]{1,0:T(8,128)S(1)}, f32[128,1024]{1,0:T(8,128)S(1)}, u32[]{:S(2)}, u32[]{:S(2)}) collective-permute-start(f32[128,1024]{1,0:T(8,128)S(1)} %collective-permute-done.8), channel_id=1, source_target_pairs={{0,2},{2,4},{4,6},{6,8},{8,10},{10,12},{12,14},{14,16},{16,18},{18... | collective-permute-start | bytes 1572872 | tf_op jit(solution)/shard_map/ppermute | solution.py:14
  92.5 15.0 %collective-permute-start.12 = (f32[256]{0:T(256)S(1)}, f32[256]{0:T(256)S(1)}, u32[]{:S(2)}, u32[]{:S(2)}) collective-permute-start(f32[256]{0:T(256)S(1)} %collective-permute-done.7), channel_id=1, source_target_pairs={{0,510},{2,0},{4,2},{6,4},{8,6},{10,8},{12,10},{14,12},{16,14},{18... | collective-permute-start | bytes 3080 | tf_op jit(solution)/shard_map/ppermute | solution.py:14
  96.9 24.7 %collective-permute-start.22 = (f32[128,1024]{1,0:T(8,128)S(1)}, f32[128,1024]{1,0:T(8,128)S(1)}, u32[]{:S(2)}, u32[]{:S(2)}) collective-permute-start(f32[128,1024]{1,0:T(8,128)S(1)} %convolution_add_fusion.7), channel_id=1, source_target_pairs={{0,2},{2,4},{4,6},{6,8},{8,10},{10,12},{12,14},{14,16},{16,18},{18... | collective-permute-start | bytes 1572872 | tf_op jit(solution)/shard_map/ppermute | solution.py:14
  101.2 29.2 %collective-permute-start.19 = (f32[256,1024]{1,0:T(8,128)S(1)}, f32[256,1024]{1,0:T(8,128)S(1)}, u32[]{:S(2)}, u32[]{:S(2)}) collective-permute-start(f32[256,1024]{1,0:T(8,128)S(1)} %collective-permute-done.14), channel_id=1, source_target_pairs={{0,510},{2,0},{4,2},{6,4},{8,6},{10,8},{12,10},{14,12},{16,14},{18... | collective-permute-start | bytes 3145736 | tf_op jit(solution)/shard_map/ppermute | solution.py:14
  110.0 21.7 %collective-permute-start.29 = (f32[256,1024]{1,0:T(8,128)S(1)}, f32[256,1024]{1,0:T(8,128)S(1)}, u32[]{:S(2)}, u32[]{:S(2)}) collective-permute-start(f32[256,1024]{1,0:T(8,128)S(1)} %convolution_add_fusion.1), channel_id=1, source_target_pairs={{0,510},{2,0},{4,2},{6,4},{8,6},{10,8},{12,10},{14,12},{16,14},{18... | collective-permute-start | bytes 3145736 | tf_op jit(solution)/shard_map/ppermute | solution.py:14
  117.8 12.5 %collective-permute-start.18 = (f32[128,1024]{1,0:T(8,128)S(1)}, f32[128,1024]{1,0:T(8,128)S(1)}, u32[]{:S(2)}, u32[]{:S(2)}) collective-permute-start(f32[128,1024]{1,0:T(8,128)S(1)} %collective-permute-done.13), channel_id=1, source_target_pairs={{0,2},{2,4},{4,6},{6,8},{8,10},{10,12},{12,14},{14,16},{16,18},{18... | collective-permute-start | bytes 1572872 | tf_op jit(solution)/shard_map/ppermute | solution.py:14
  125.9 10.5 %collective-permute-start.23 = (f32[128,1024]{1,0:T(8,128)S(1)}, f32[128,1024]{1,0:T(8,128)S(1)}, u32[]{:S(2)}, u32[]{:S(2)}) collective-permute-start(f32[128,1024]{1,0:T(8,128)S(1)} %convolution_add_fusion.6), channel_id=1, source_target_pairs={{0,2},{2,4},{4,6},{6,8},{8,10},{10,12},{12,14},{14,16},{16,18},{18... | collective-permute-start | bytes 1572872 | tf_op jit(solution)/shard_map/ppermute | solution.py:14
  132.8 29.1 %collective-permute-start.30 = (f32[256,1024]{1,0:T(8,128)S(1)}, f32[256,1024]{1,0:T(8,128)}, u32[]{:S(2)}, u32[]{:S(2)}) collective-permute-start(f32[256,1024]{1,0:T(8,128)S(1)} %convolution_add_fusion), channel_id=1, source_target_pairs={{0,8},{2,10},{4,12},{6,14},{8,16},{10,18},{12,20},{14,22},{16,24},... | collective-permute-start | bytes 3145736 | tf_op jit(solution)/shard_map/ppermute | solution.py:14
  137.2 28.7 %collective-permute-start.24 = (f32[128,1024]{1,0:T(8,128)S(1)}, f32[128,1024]{1,0:T(8,128)}, u32[]{:S(2)}, u32[]{:S(2)}) collective-permute-start(f32[128,1024]{1,0:T(8,128)S(1)} %convolution_add_fusion.5), channel_id=1, source_target_pairs={{0,2},{2,4},{4,6},{6,8},{8,10},{10,12},{12,14},{14,16},{16,18},{18... | collective-permute-start | bytes 1572872 | tf_op jit(solution)/shard_map/ppermute | solution.py:14
  167.7 52.1 %collective-permute-start.25 = (f32[128,1024]{1,0:T(8,128)S(1)}, f32[128,1024]{1,0:T(8,128)S(1)}, u32[]{:S(2)}, u32[]{:S(2)}) collective-permute-start(f32[128,1024]{1,0:T(8,128)S(1)} %convolution_add_fusion.4), channel_id=1, source_target_pairs={{0,504},{2,506},{4,508},{6,510},{8,0},{10,2},{12,4},{14,6},{16,8},... | collective-permute-start | bytes 1572872 | tf_op jit(solution)/shard_map/ppermute | solution.py:14
  171.9 14.4 %collective-permute-start = (f32[128]{0:T(128)S(1)}, f32[128]{0:T(128)S(1)}, u32[]{:S(2)}, u32[]{:S(2)}) collective-permute-start(f32[128]{0:T(128)S(1)} %get-tuple-element.3), channel_id=1, source_target_pairs={{0,2},{2,4},{4,6},{6,8},{8,10},{10,12},{12,14},{14,16},{16,18},{18... | collective-permute-start | bytes 1544 | tf_op jit(solution)/shard_map/ppermute | solution.py:14
  (14 other events, 106.6 us)
Sparse Core Ops, SparseCore 0:
  162.0 69.1 all-reduce.1
where the time goes:
time: 242 us; the launch traced here: 241 us
  starting transfers between devices  129 us (53%)
  waiting for transfers between devices  69.1 us (29%)
  matrix products  19.4 us (8%)
  between operations  15.9 us (7%)
  other arithmetic  6.33 us (3%)
    ppermute x31, starting transfers between devices, passed_along(): lax.ppermute(x, axis, [(i, (i + by) % length) for i in range(length)])  129 us
    ppermute x31, waiting for transfers between devices, passed_along(): lax.ppermute(x, axis, [(i, (i + by) % length) for i in range(length)])  58.8 us
    psum x1, waiting for transfers between devices, finish_struct(): return lax.psum(summed, 'rep')  10.3 us
    dot_general x5, matrix products, pairwise_tile(): lax.dot_general(residue_string_entries, fold_shape_entries, (((1,), (1,))...  7.88 us
    dot_general x5, matrix products, pairwise_tile(): jnp.dot(weight, fold_shape_entries, precision=lax.Precision.HIGHEST, pref...  5.99 us
    dot_general x5, matrix products, pairwise_tile(): lax.dot_general(weight, residue_string_entries, (((0,), (0,)), ((), ())),...  5.49 us
  transfers between devices with their start and end apart: 32, of which 10 were waited for; matrix products, arithmetic and copies ran while one was open for 9% of the time, Pallas kernels for 0%

commit v1 on v0

v1 whole, which is shorter than its diff:
```python
import functools

import jax
import jax.numpy as jnp
from jax import lax
from jax.experimental import pallas as pl
from jax.experimental.pallas import tpu as pltpu
from jax.sharding import PartitionSpec as P

MESH = pl.DeviceIdType.MESH
HOPS = 4
EPSILON = 1e-06
CHUNKS = 4
RING = 4
TILES = (1, 3, 2)


def split(value):
    high = value.astype(jnp.bfloat16)
    return high, (value - high.astype(jnp.float32)).astype(jnp.bfloat16)


def dot3(a, b, dims):
    def one(p, q):
        return lax.dot_general(p, q, (dims, ((), ())), preferred_element_type=jnp.float32)

    return one(a[0], b[0]) + one(a[0], b[1]) + one(a[1], b[0])


def unit_of(raw):
    length = jnp.sqrt(jnp.sum(raw * raw, axis=1, keepdims=True) + EPSILON)
    return raw / length, length


def project(direction, raw):
    unit, length = unit_of(raw)
    along = jnp.sum(unit * direction, axis=1, keepdims=True)
    return (direction - unit * along) / length


def kernel(
    groups,
    seq_hbm,
    st_hbm,
    lab_ref,
    scale_ref,
    bias_ref,
    loss_out,
    seq_out,
    st_out,
    seqv,
    units,
    labs,
    parts,
    backs,
    cross_back,
    acc,
    seq_part,
    loss_mine,
    loss_part,
    final,
    sq_hi,
    sq_lo,
    load_sem,
    seq_sems,
    loss_sems,
    sp_sems,
    cross_s,
    cross_r,
    ring_s,
    ring_r,
    lab_s,
    lab_r,
    back_s,
    back_r,
    xback_s,
    xback_r,
    final_s,
    final_r,
):
    half = seq_hbm.shape[0]
    rows = half // CHUNKS
    blk, rep = lax.axis_index("blk"), lax.axis_index("rep")
    core, x, group = blk % 2, (blk // 2) % RING, blk // (2 * RING)

    def at(g, column, replica):
        return ((lax.rem(g + groups, groups) * RING + lax.rem(column + RING, RING)) * 2 + core, replica)

    def ring(by):
        return at(group, x + by, rep)

    up = at(group + 1, x, lax.rem(rep + group + core, 2))
    down = at(group - 1, x, lax.rem(rep + group + 1 + core, 2))
    partner = (blk, 1 - rep)

    def send(src, dst, send_sem, recv_sem, device):
        return pltpu.make_async_remote_copy(
            src_ref=src, dst_ref=dst, send_sem=send_sem, recv_sem=recv_sem, device_id=device, device_id_type=MESH
        )

    def part(k):
        return pl.ds(k * rows, rows)

    mine = pl.multiple_of(rep * half, half)

    def source(k):
        return st_hbm.at[pl.ds(mine + k * rows, rows)]

    def cross_copy(k):
        return send(source(k), units.at[HOPS, part(k)], cross_s.at[k], cross_r.at[k], down)

    def ring_copy(h, k, crossed):
        src = units.at[HOPS, part(k)] if crossed else source(k)
        return send(src, units.at[h, part(k)], ring_s.at[h - 1, k], ring_r.at[h - 1, k], ring(-h))

    def label_copy(h, crossed):
        src = labs.at[HOPS if crossed else 0]
        return send(src, labs.at[h], lab_s.at[h - 1], lab_r.at[h - 1], down if h == HOPS else ring(-h))

    def back_copy(h, k):
        return send(parts.at[h, part(k)], backs.at[h - 1, part(k)], back_s.at[h - 1, k], back_r.at[h - 1, k], ring(h))

    def cross_back_copy(k):
        return send(parts.at[HOPS, part(k)], cross_back.at[part(k)], xback_s.at[k], xback_r.at[k], up)

    def final_copy(k):
        return send(parts.at[0, part(k)], final.at[part(k)], final_s.at[k], final_r.at[k], partner)

    seq_copy = send(seq_hbm, seqv.at[pl.ds(half, half)], seq_sems.at[0], seq_sems.at[1], partner)
    seq_part_copy = send(acc.at[pl.ds(half, half)], seq_part, sp_sems.at[0], sp_sems.at[1], partner)
    loss_copy = send(loss_mine, loss_part, loss_sems.at[0], loss_sems.at[1], partner)

    load_seq = pltpu.make_async_copy(seq_hbm, seqv.at[pl.ds(0, half)], load_sem.at[0])
    load_st = pltpu.make_async_copy(st_hbm.at[pl.ds(mine, half)], units.at[0], load_sem.at[1])
    load_seq.start()
    load_st.start()

    barrier = pltpu.get_barrier_semaphore()
    for device in (ring(1), ring(2), ring(3), up, down, partner):
        pl.semaphore_signal(barrier, 1, device_id=device, device_id_type=MESH)
    my_labels = lab_ref[pl.ds(rep, 1), :]
    other_labels = lab_ref[pl.ds(1 - rep, 1), :]
    labs[0] = jnp.broadcast_to(my_labels, (8, half))
    pl.semaphore_wait(barrier, 6)

    for k in range(CHUNKS):
        cross_copy(k).start()
    label_copy(HOPS, False).start()
    for h in TILES:

        @pl.when(x >= h)
        def _():
            for k in range(CHUNKS):
                ring_copy(h, k, False).start()
            label_copy(h, False).start()

    seq_copy.start()

    load_seq.wait()
    unit, _ = unit_of(seqv[pl.ds(0, half)])
    sq_hi[pl.ds(0, half)], sq_lo[pl.ds(0, half)] = split(unit)
    load_st.wait()

    for k in range(CHUNKS):
        cross_copy(k).wait_recv()
        for h in TILES:

            @pl.when(x < h)
            def _():
                ring_copy(h, k, True).start()

    label_copy(HOPS, False).wait_recv()
    for h in TILES:

        @pl.when(x < h)
        def _():
            label_copy(h, True).start()

    seq_copy.wait_recv()
    unit, _ = unit_of(seqv[pl.ds(half, half)])
    sq_hi[pl.ds(half, half)], sq_lo[pl.ds(half, half)] = split(unit)

    scale, bias = scale_ref[0], bias_ref[0]

    def tile(h, first, loss):
        st = split(unit_of(units[h])[0])
        sq = (sq_hi[...], sq_lo[...])
        logit = scale * dot3(st, sq, ((1,), (1,))) + bias
        label = jnp.broadcast_to(labs[h][0:1, :].astype(jnp.float32), (half, half)).T
        match = jnp.concatenate(
            [label == my_labels.astype(jnp.float32), label == other_labels.astype(jnp.float32)], axis=1
        )
        margin = jnp.where(match, -logit, logit)
        small = jnp.exp(-jnp.abs(margin))
        loss = loss + jnp.sum(jnp.maximum(margin, 0.0) + jnp.log1p(small), axis=0, keepdims=True)
        sigmoid = jnp.where(margin >= 0.0, 1.0, small) / (1.0 + small)
        weight = jnp.where(match, -sigmoid, sigmoid)
        parts[h] = dot3(split(weight), sq, ((1,), (0,)))
        towards = dot3(split(weight.T), st, ((1,), (0,)))
        if first:
            acc[...] = towards
        else:
            acc[...] += towards
        return loss

    loss = jnp.zeros((1, 2 * half), jnp.float32)
    loss = tile(0, True, loss)
    loss = tile(HOPS, False, loss)
    for h in TILES:
        for k in range(CHUNKS):
            ring_copy(h, k, False).wait_recv()
        label_copy(h, False).wait_recv()
        loss = tile(h, False, loss)
        for k in range(CHUNKS):
            back_copy(h, k).start()

    seq_part_copy.start()
    loss_mine[...] = jnp.broadcast_to(loss[:, half:], (8, half))
    loss_copy.start()

    def collect(k):
        for h in TILES:

            @pl.when(x < h)
            def _():
                back_copy(h, k).wait_recv()
                parts[HOPS, part(k)] += backs[h - 1, part(k)]

        cross_back_copy(k).start()

    def finish(k):
        for h in TILES:

            @pl.when(x >= h)
            def _():
                back_copy(h, k).wait_recv()
                parts[0, part(k)] += backs[h - 1, part(k)]

        cross_back_copy(k).wait_recv()
        direction = scale * (parts[0, part(k)] + cross_back[part(k)])
        done = project(direction, units[0, part(k)])
        parts[0, part(k)] = done
        final_copy(k).start()
        st_out[pl.ds(mine + k * rows, rows)] = done

    for k in range(CHUNKS + 1):
        if k < CHUNKS:
            collect(k)
        if k > 0:
            finish(k - 1)

    loss_copy.wait_recv()
    loss_out[...] = (loss[:, :half] + loss_part[0:1, :]) / ((HOPS + 1) * 2.0 * half)
    seq_part_copy.wait_recv()
    seq_out[...] = project(scale * (acc[pl.ds(0, half)] + seq_part[...]), seqv[pl.ds(0, half)])

    theirs = pl.multiple_of((1 - rep) * half, half)
    for k in range(CHUNKS):
        final_copy(k).wait_recv()
        st_out[pl.ds(theirs + k * rows, rows)] = final[part(k)]

    for k in range(CHUNKS):
        cross_copy(k).wait_send()
        cross_back_copy(k).wait_send()
        final_copy(k).wait_send()
        for h in TILES:
            ring_copy(h, k, False).wait_send()
            back_copy(h, k).wait_send()
    for h in TILES + (HOPS,):
        label_copy(h, False).wait_send()
    seq_copy.wait_send()
    seq_part_copy.wait_send()
    loss_copy.wait_send()


def body(seq, st, label, scale, bias):
    half, features = seq.shape
    f32, bf16 = jnp.float32, jnp.bfloat16
    vmem, dma = pltpu.VMEM, pltpu.SemaphoreType.DMA
    groups = lax.axis_size("blk") // (2 * RING)
    loss, seq_grad, st_grad = pl.pallas_call(
        functools.partial(kernel, groups),
        out_shape=(
            jax.ShapeDtypeStruct((1, half), f32),
            jax.ShapeDtypeStruct(seq.shape, f32),
            jax.ShapeDtypeStruct(st.shape, f32),
        ),
        in_specs=[
            pl.BlockSpec(memory_space=pl.ANY),
            pl.BlockSpec(memory_space=pl.ANY),
            pl.BlockSpec(memory_space=vmem),
            pl.BlockSpec(memory_space=pltpu.SMEM),
            pl.BlockSpec(memory_space=pltpu.SMEM),
        ],
        out_specs=(pl.BlockSpec(memory_space=vmem),) * 3,
        scratch_shapes=[
            vmem((2 * half, features), f32),
            vmem((HOPS + 1, half, features), f32),
            vmem((HOPS + 1, 8, half), jnp.int32),
            vmem((HOPS + 1, half, features), f32),
            vmem((RING - 1, half, features), f32),
            vmem((half, features), f32),
            vmem((2 * half, features), f32),
            vmem((half, features), f32),
            vmem((8, half), f32),
            vmem((8, half), f32),
            vmem((half, features), f32),
            vmem((2 * half, features), bf16),
            vmem((2 * half, features), bf16),
            dma((2,)),
            dma((2,)),
            dma((2,)),
            dma((2,)),
            dma((CHUNKS,)),
            dma((CHUNKS,)),
            dma((RING - 1, CHUNKS)),
            dma((RING - 1, CHUNKS)),
            dma((HOPS,)),
            dma((HOPS,)),
            dma((RING - 1, CHUNKS)),
            dma((RING - 1, CHUNKS)),
            dma((CHUNKS,)),
            dma((CHUNKS,)),
            dma((CHUNKS,)),
            dma((CHUNKS,)),
        ],
        compiler_params=pltpu.CompilerParams(
            collective_id=1, has_side_effects=True, vmem_limit_bytes=56 * 2**20
        ),
    )(seq, st, label.reshape(2, half), scale, bias)
    return loss.reshape(half), seq_grad, st_grad


def solution(mesh):
    placed = (P(("blk", "rep"), None), P("blk", None), P("blk"), P(), P())
    return jax.shard_map(
        body,
        mesh=mesh,
        in_specs=placed,
        out_specs=(P(("blk", "rep")), P(("blk", "rep"), None), P("blk", None)),
        check_vma=False,
    )
```

time: 242 us -> 95.1 us (0.39)
  the two profiles are of different devices: /device:TPU:1 before, /device:TPU:26 now
where the time goes in v1:
time: 95.1 us; the launch traced here: 94.9 us
  Pallas kernels  88.9 us (93%)
  local copies, waits for them, and re-layouts  4.08 us (4%)
  between operations  1.94 us (2%)
    pallas_call x1, Pallas kernels, body(): pl.pallas_call(functools.partial(kernel, groups), out_shape=(jax.ShapeDty...  88.9 us
    unnamed x5, local copies, waits for them, and re-layouts  4.08 us

profile of v1, /device:TPU:26, one launch (start us, length us, event | category | flops | bytes accessed | tf_op | source)
XLA Modules:
  0.0 94.9 jit_solution(4664574966332895560)
XLA Ops:
  1.9 88.9 %shard_map.76 = (f32[1,128]{1,0:T(1,128)}, f32[128,1024]{1,0:T(8,128)}, f32[256,1024]{1,0:T(8,128)}) custom-call(f32[128,1024]{1,0:T(8,128)} %seq_hbm.1, f32[256,1024]{1,0:T(8,128)} %st_hbm.1, s32[2,128]{1,0:T(2,128)} %bitcast.2, f32[1]{0:T(128)S(6)} %copy.11.scale_ref, f32[1]{0:T(128)S(6)} %copy.12.bias_ref), custom_call_target="tpu_custom_call" | custom-call | tf_op jit(solution)/shard_map/pallas_call | solution.py:281
  90.8 0.0 copy-start
  90.8 1.2 %copy.13 = f32[128]{0:T(128)} copy(f32[128]{0:T(128)} %bitcast.3) | data formatting | bytes 1024
  92.0 1.9 %copy.14 = f32[128,1024]{1,0:T(8,128)} copy(f32[128,1024]{1,0:T(8,128)} %get-tuple-element.13) | data formatting | bytes 1048576
  93.9 0.0 copy-done
  93.9 1.0 %copy.15 = f32[256,1024]{1,0:T(8,128)} copy(f32[256,1024]{1,0:T(8,128)S(1)} %copy-done) | data formatting | bytes 2097152
Async XLA Ops:
  90.8 3.1 %copy-start = (f32[256,1024]{1,0:T(8,128)S(1)}, f32[256,1024]{1,0:T(8,128)}, u32[]{:S(2)}) copy-start(f32[256,1024]{1,0:T(8,128)} %get-tuple-element.14) | copy-start | bytes 3145732

commit v2 on v1

v2 whole, which is shorter than its diff:
```python
import functools

import jax
import jax.numpy as jnp
from jax import lax
from jax.experimental import pallas as pl
from jax.experimental.pallas import tpu as pltpu
from jax.sharding import PartitionSpec as P

MESH = pl.DeviceIdType.MESH
HOPS = 4
EPSILON = 1e-06
CHUNKS = 4
RING = 4
TILES = (3, 2, 1)
PIECES = 4
RELAY = True
READY = 4


def split(value):
    high = value.astype(jnp.bfloat16)
    return high, (value - high.astype(jnp.float32)).astype(jnp.bfloat16)


def dot3(a, b, dims):
    def one(p, q):
        return lax.dot_general(p, q, (dims, ((), ())), preferred_element_type=jnp.float32)

    return one(a[0], b[0]) + one(a[0], b[1]) + one(a[1], b[0])


def unit_of(raw):
    length = jnp.sqrt(jnp.sum(raw * raw, axis=1, keepdims=True) + EPSILON)
    inverse = 1.0 / length
    return raw * inverse, inverse


def project(direction, raw):
    unit, inverse = unit_of(raw)
    along = jnp.sum(unit * direction, axis=1, keepdims=True)
    return (direction - unit * along) * inverse


def kernel(
    groups,
    seq_hbm,
    st_hbm,
    lab_ref,
    scale_ref,
    bias_ref,
    loss_hbm,
    seq_out,
    st_out,
    stv,
    units,
    labs,
    columns,
    parts,
    backs,
    cross_back,
    acc,
    acc_in,
    losses,
    loss_backs,
    loss_cross,
    st_hi,
    st_lo,
    load_sem,
    acc_s,
    acc_r,
    cross_s,
    cross_r,
    ring_s,
    ring_r,
    lab_s,
    lab_r,
    back_s,
    back_r,
    xback_s,
    xback_r,
    loss_s,
    loss_r,
    loss_out,
    put_sem,
):
    half, features = seq_hbm.shape
    rows = half // CHUNKS
    piece = 2 * half // PIECES
    blk, rep = lax.axis_index("blk"), lax.axis_index("rep")
    core, x, group = blk % 2, (blk // 2) % RING, blk // (2 * RING)

    def at(g, column, replica):
        return ((lax.rem(g + groups, groups) * RING + lax.rem(column + RING, RING)) * 2 + core, replica)

    def ring(by):
        return at(group, x + by, rep)

    rep_up = lax.rem(rep + group + core, 2)
    rep_down = lax.rem(rep + group + 1 + core, 2)
    up = at(group + 1, x, rep_up)
    down = at(group - 1, x, rep_down)
    wraps = jnp.where(x == RING - 1, 1, 0)
    later = at(group + wraps, x + 1, jnp.where(x == RING - 1, rep_up, rep))
    wraps = jnp.where(x == 0, 1, 0)
    earlier = at(group - wraps, x - 1, jnp.where(x == 0, rep_down, rep))
    partner = (blk, 1 - rep)

    def send(src, dst, send_sem, recv_sem, device):
        return pltpu.make_async_remote_copy(
            src_ref=src, dst_ref=dst, send_sem=send_sem, recv_sem=recv_sem, device_id=device, device_id_type=MESH
        )

    def stays(h):
        return x < RING - h

    def leaves(h):
        return x >= RING - h

    def source(k):
        return seq_hbm.at[pl.ds(k * rows, rows)]

    def cross_copy(k):
        return send(source(k), units.at[k, HOPS], cross_s.at[k], cross_r.at[k], up)

    def ring_copy(h, k, crossed):
        src = units.at[k, HOPS] if crossed else source(k)
        return send(src, units.at[k, h], ring_s.at[h - 1, k], ring_r.at[h - 1, k], ring(h))

    def second_copy(k):
        over = k % 2 == 0
        return send(
            units.at[k, 1 if over else 3], units.at[k, 2], ring_s.at[1, k], ring_r.at[1, k], later if over else earlier
        )

    def label_copy(h, crossed):
        src = labs.at[HOPS if crossed else 0]
        return send(src, labs.at[h], lab_s.at[h - 1], lab_r.at[h - 1], up if h == HOPS else ring(h))

    def back_copy(h, k):
        return send(parts.at[k, h], backs.at[k, h - 1], back_s.at[h - 1, k], back_r.at[h - 1, k], ring(-h))

    def cross_back_copy(k):
        return send(parts.at[k, HOPS], cross_back.at[k], xback_s.at[k], xback_r.at[k], down)

    def loss_copy(h):
        dst = loss_cross if h == HOPS else loss_backs.at[h - 1]
        return send(losses.at[h], dst, loss_s.at[h - 1], loss_r.at[h - 1], down if h == HOPS else ring(-h))

    def acc_copy(p):
        here = pl.ds(p * piece, piece)
        return send(acc.at[here], acc_in.at[here], acc_s.at[p], acc_r.at[p], partner)

    load_st = pltpu.make_async_copy(st_hbm, stv, load_sem.at[0])
    load_seq = [pltpu.make_async_copy(source(k), units.at[k, 0], load_sem.at[1 + k]) for k in range(CHUNKS)]
    load_st.start()
    for copy in load_seq:
        copy.start()

    barrier = pltpu.get_barrier_semaphore()
    greeted = (ring(1), ring(2), ring(3), up, down, partner, later, earlier)
    for device in greeted:
        pl.semaphore_signal(barrier, 1, device_id=device, device_id_type=MESH)
    labs[0] = jnp.broadcast_to(lab_ref[pl.ds(rep, 1), :], (8, half))
    label_rows = [lab_ref[q : q + 1, :].astype(jnp.float32) for q in range(2)]
    pl.semaphore_wait(barrier, len(greeted))

    direct = (1, 3) if RELAY else (1, 3, 2)

    def forward(k):
        for h in direct:

            @pl.when(stays(h))
            def _():
                ring_copy(h, k, False).start()

    def relay(k):
        cross_copy(k).wait_recv()
        for h in direct:

            @pl.when(leaves(h))
            def _():
                ring_copy(h, k, True).start()

    def second(k):
        ring_copy(1 if k % 2 == 0 else 3, k, False).wait_recv()
        second_copy(k).start()

    def arrived(k):
        for h in TILES:
            if not (RELAY and h == (1 if k % 2 == 0 else 3)):
                ring_copy(h, k, False).wait_recv()

    def column(h):
        tall = jnp.broadcast_to(labs[h][0:1, :].astype(jnp.float32), (half, half)).T
        for k in range(CHUNKS):
            columns[k, h] = tall[k * rows : (k + 1) * rows]

    scale, bias = scale_ref[0], bias_ref[0]

    def back(k):
        for h in TILES:
            back_copy(h, k).start()

    def stage(k):
        arrived(k)
        seq = split(unit_of(units[k].reshape((HOPS + 1) * rows, features))[0])
        st = (st_hi[...], st_lo[...])
        logit = scale * dot3(seq, st, ((1,), (1,))) + bias
        label = columns[k].reshape((HOPS + 1) * rows, half)
        match = jnp.concatenate([label == label_rows[0], label == label_rows[1]], axis=1)
        margin = jnp.where(match, -logit, logit)
        small = jnp.exp(-jnp.abs(margin))
        loss = jnp.sum(jnp.maximum(margin, 0.0) + jnp.log1p(small), axis=1, keepdims=True)
        loss = jnp.broadcast_to(loss, label.shape).reshape(HOPS + 1, rows, half)
        columns[k] = loss
        sigmoid = jnp.where(margin >= 0.0, 1.0, small) / (1.0 + small)
        weight = split(jnp.where(match, -sigmoid, sigmoid))
        parts[k] = dot3(weight, st, ((1,), (0,))).reshape(HOPS + 1, rows, features)
        back(k)
        towards = lax.dot_general(
            jnp.concatenate([weight[0], weight[1], weight[0]], axis=0),
            jnp.concatenate([seq[0], seq[0], seq[1]], axis=0),
            (((0,), (0,)), ((), ())),
            preferred_element_type=jnp.float32,
        )
        if k == 0:
            acc[...] = towards
        else:
            acc[...] += towards

    def collect(k):
        for h in TILES:

            @pl.when(leaves(h))
            def _():
                back_copy(h, k).wait_recv()
                parts[k, HOPS] += backs[k, h - 1]

        cross_back_copy(k).start()

    def finish(k):
        for h in TILES:

            @pl.when(stays(h))
            def _():
                back_copy(h, k).wait_recv()
                parts[k, 0] += backs[k, h - 1]

        cross_back_copy(k).wait_recv()
        parts[k, 0] = project(scale * (parts[k, 0] + cross_back[k]), units[k, 0])
        put_seq(k).start()

    put_loss = pltpu.make_async_copy(loss_out, loss_hbm, put_sem.at[0])

    def put_seq(k):
        return pltpu.make_async_copy(parts.at[k, 0], seq_out.at[pl.ds(k * rows, rows)], put_sem.at[1 + k])

    def put_st(p):
        here = pl.ds(p * piece, piece)
        return pltpu.make_async_copy(acc_in.at[here], st_out.at[here], put_sem.at[1 + CHUNKS + p])

    def settle(p):
        here = pl.ds(p * piece, piece)
        acc_copy(p).wait_recv()
        acc_in[here] = project(scale * (acc[here] + acc_in[here]), stv[here])
        put_st(p).start()

    label_copy(HOPS, False).start()
    for h in TILES:

        @pl.when(stays(h))
        def _():
            label_copy(h, False).start()

    for k in range(CHUNKS):
        cross_copy(k).start()
        forward(k)

    column(0)
    load_st.wait()
    unit, _ = unit_of(stv[...])
    st_hi[...], st_lo[...] = split(unit)
    for copy in load_seq:
        copy.wait()
    label_copy(HOPS, False).wait_recv()
    for h in TILES:

        @pl.when(leaves(h))
        def _():
            label_copy(h, True).start()

    column(HOPS)
    for k in range(CHUNKS):
        relay(k)
    for h in TILES:
        label_copy(h, False).wait_recv()
        column(h)
    for k in range(READY if RELAY else 0):
        second(k)
    for k in range(CHUNKS):
        stage(k)
        if RELAY and k + READY < CHUNKS:
            second(k + READY)
    for p in range(PIECES):
        acc_copy(p).start()

    for h in range(HOPS + 1):
        tall = jnp.concatenate([columns[k, h] for k in range(CHUNKS)], axis=0)
        losses[h] = tall.T[0:8, :]
    for h in TILES:
        loss_copy(h).start()
    for k in range(CHUNKS):
        collect(k)
        if k == 1:
            for h in TILES:
                loss_copy(h).wait_recv()
            gone = losses[HOPS]
            kept = losses[0]
            for h in TILES:
                gone += jnp.where(leaves(h), loss_backs[h - 1], 0.0)
                kept += jnp.where(stays(h), loss_backs[h - 1], 0.0)
            losses[HOPS] = gone
            loss_copy(HOPS).start()
    for p in range(PIECES):
        settle(p)
    for k in range(CHUNKS):
        finish(k)
    loss_copy(HOPS).wait_recv()
    loss_out[...] = (kept[0:1, :] + loss_cross[0:1, :]) / ((HOPS + 1) * 2.0 * half)
    put_loss.start()

    for k in range(CHUNKS):
        cross_copy(k).wait_send()
        cross_back_copy(k).wait_send()
        for h in TILES:
            ring_copy(h, k, False).wait_send()
            back_copy(h, k).wait_send()
    for h in TILES + (HOPS,):
        label_copy(h, False).wait_send()
        loss_copy(h).wait_send()
    for p in range(PIECES):
        acc_copy(p).wait_send()
        put_st(p).wait()
    for k in range(CHUNKS):
        put_seq(k).wait()
    put_loss.wait()


def hand_over(a, b, c, p, q, r, sa, sb, sc, sem):
    moves = [(a, sa, p, slice(None)), (b, sb, q, slice(None))]
    half = b.shape[0]
    moves += [(c, sc, r, pl.ds(i * half, half)) for i in range(2)]
    ins = [pltpu.make_async_copy(s.at[w], v.at[w], sem.at[0, i]) for i, (s, v, _, w) in enumerate(moves)]
    outs = [pltpu.make_async_copy(v.at[w], d.at[w], sem.at[1, i]) for i, (_, v, d, w) in enumerate(moves)]
    for copy in ins:
        copy.start()
    for into, out in zip(ins, outs):
        into.wait()
        out.start()
    for copy in outs:
        copy.wait()


def body(seq, st, label, scale, bias):
    half, features = seq.shape
    rows = half // CHUNKS
    f32, bf16 = jnp.float32, jnp.bfloat16
    vmem, dma = pltpu.VMEM, pltpu.SemaphoreType.DMA
    groups = lax.axis_size("blk") // (2 * RING)
    loss, seq_grad, st_grad = pl.pallas_call(
        functools.partial(kernel, groups),
        out_shape=(
            jax.ShapeDtypeStruct((1, half), f32),
            jax.ShapeDtypeStruct(seq.shape, f32),
            jax.ShapeDtypeStruct(st.shape, f32),
        ),
        in_specs=[
            pl.BlockSpec(memory_space=pl.ANY),
            pl.BlockSpec(memory_space=pl.ANY),
            pl.BlockSpec(memory_space=vmem),
            pl.BlockSpec(memory_space=pltpu.SMEM),
            pl.BlockSpec(memory_space=pltpu.SMEM),
        ],
        out_specs=(pl.BlockSpec(memory_space=pl.ANY),) * 3,
        scratch_shapes=[
            vmem((2 * half, features), f32),
            vmem((CHUNKS, HOPS + 1, rows, features), f32),
            vmem((HOPS + 1, 8, half), jnp.int32),
            vmem((CHUNKS, HOPS + 1, rows, half), f32),
            vmem((CHUNKS, HOPS + 1, rows, features), f32),
            vmem((CHUNKS, RING - 1, rows, features), f32),
            vmem((CHUNKS, rows, features), f32),
            vmem((2 * half, features), f32),
            vmem((2 * half, features), f32),
            vmem((HOPS + 1, 8, half), f32),
            vmem((RING - 1, 8, half), f32),
            vmem((8, half), f32),
            vmem((2 * half, features), bf16),
            vmem((2 * half, features), bf16),
            dma((1 + CHUNKS,)),
            dma((PIECES,)),
            dma((PIECES,)),
            dma((CHUNKS,)),
            dma((CHUNKS,)),
            dma((RING - 1, CHUNKS)),
            dma((RING - 1, CHUNKS)),
            dma((HOPS,)),
            dma((HOPS,)),
            dma((RING - 1, CHUNKS)),
            dma((RING - 1, CHUNKS)),
            dma((CHUNKS,)),
            dma((CHUNKS,)),
            dma((HOPS,)),
            dma((HOPS,)),
            vmem((1, half), f32),
            dma((1 + CHUNKS + PIECES,)),
        ],
        compiler_params=pltpu.CompilerParams(
            collective_id=1, has_side_effects=True, vmem_limit_bytes=56 * 2**20
        ),
    )(seq, st, label.reshape(2, half), scale, bias)
    loss, seq_grad, st_grad = pl.pallas_call(
        hand_over,
        out_shape=(
            jax.ShapeDtypeStruct((1, half), f32),
            jax.ShapeDtypeStruct(seq.shape, f32),
            jax.ShapeDtypeStruct(st.shape, f32),
        ),
        in_specs=[pl.BlockSpec(memory_space=pl.ANY)] * 3,
        out_specs=(pl.BlockSpec(memory_space=pl.ANY),) * 3,
        scratch_shapes=[vmem((1, half), f32), vmem(seq.shape, f32), vmem(st.shape, f32), dma((2, 4))],
        name="hand_over",
    )(loss, seq_grad, st_grad)
    return loss.reshape(half), seq_grad, st_grad


def solution(mesh):
    placed = (P(("blk", "rep"), None), P("blk", None), P("blk"), P(), P())
    return jax.shard_map(
        body,
        mesh=mesh,
        in_specs=placed,
        out_specs=(P(("blk", "rep")), P(("blk", "rep"), None), P("blk", None)),
        check_vma=False,
    )
```

time: 95.1 us -> 81 us (0.85)
  the two profiles are of different devices: /device:TPU:26 before, /device:TPU:16 now
where the time goes in v2:
time: 81 us; the launch traced here: 80.8 us
  Pallas kernels  78.9 us (97%)
  between operations  1.93 us (2%)
    pallas_call x1, Pallas kernels, body(): pl.pallas_call(functools.partial(kernel, groups), out_shape=(jax.ShapeDty...  76.6 us
    pallas_call x1, Pallas kernels, body(): pl.pallas_call(hand_over, out_shape=(jax.ShapeDtypeStruct((1, half), f32)...  2.25 us

profile of v2, /device:TPU:16, one launch (start us, length us, event | category | flops | bytes accessed | tf_op | source)
XLA Modules:
  0.0 80.8 jit_solution(12526008607182472121)
XLA Ops:
  1.9 76.6 %shard_map.76 = (f32[1,128]{1,0:T(1,128)}, f32[128,1024]{1,0:T(8,128)}, f32[256,1024]{1,0:T(8,128)}) custom-call(f32[128,1024]{1,0:T(8,128)} %seq_hbm.1, f32[256,1024]{1,0:T(8,128)} %st_hbm.1, s32[2,128]{1,0:T(2,128)} %bitcast.2, f32[1]{0:T(128)S(6)} %copy.8.scale_ref, f32[1]{0:T(128)S(6)} %copy.9.bias_ref), custom_call_target="tpu_custom_call" | custom-call | tf_op jit(solution)/shard_map/pallas_call | solution.py:371
  78.6 2.3 %hand_over.1 = (f32[1,128]{1,0:T(1,128)}, f32[128,1024]{1,0:T(8,128)}, f32[256,1024]{1,0:T(8,128)}) custom-call(f32[1,128]{1,0:T(1,128)} %get-tuple-element.9.a, f32[128,1024]{1,0:T(8,128)} %get-tuple-element.10.b, f32[256,1024]{1,0:T(8,128)} %get-tuple-element.11.c), custom_call_target="tpu_custom_call" | custom-call | tf_op jit(solution)/shard_map/hand_over/pallas_call | solution.py:423

commit v3 on v2

--- a/solution.py
+++ b/solution.py
@@ -14,8 +14,8 @@
 RING = 4
 TILES = (3, 2, 1)
 PIECES = 4
-RELAY = True
-READY = 4
+FINE = 8
+FOURTH = 4
 
 
 def split(value):
@@ -120,18 +120,28 @@
     def source(k):
         return seq_hbm.at[pl.ds(k * rows, rows)]
 
-    def cross_copy(k):
-        return send(source(k), units.at[k, HOPS], cross_s.at[k], cross_r.at[k], up)
-
-    def ring_copy(h, k, crossed):
-        src = units.at[k, HOPS] if crossed else source(k)
-        return send(src, units.at[k, h], ring_s.at[h - 1, k], ring_r.at[h - 1, k], ring(h))
-
-    def second_copy(k):
-        over = k % 2 == 0
-        return send(
-            units.at[k, 1 if over else 3], units.at[k, 2], ring_s.at[1, k], ring_r.at[1, k], later if over else earlier
-        )
+    fine = half // FINE
+
+    def fresh(j):
+        return seq_hbm.at[pl.ds(j * fine, fine)]
+
+    def visitor(h, j):
+        per = FINE // CHUNKS
+        return units.at[j // per, h, pl.ds((j % per) * fine, fine)]
+
+    def cross_copy(j):
+        return send(fresh(j), visitor(HOPS, j), cross_s.at[j], cross_r.at[j], up)
+
+    def ring_copy(h, j, crossed):
+        src = visitor(HOPS, j) if crossed else fresh(j)
+        return send(src, visitor(h, j), ring_s.at[h - 1, j], ring_r.at[h - 1, j], ring(h))
+
+    def via(j):
+        return 1 if j % 2 == 0 else 3
+
+    def second_copy(j):
+        device = later if via(j) == 1 else earlier
+        return send(visitor(via(j), j), visitor(2, j), ring_s.at[1, j], ring_r.at[1, j], device)
 
     def label_copy(h, crossed):
         src = labs.at[HOPS if crossed else 0]
@@ -165,7 +175,7 @@
     label_rows = [lab_ref[q : q + 1, :].astype(jnp.float32) for q in range(2)]
     pl.semaphore_wait(barrier, len(greeted))
 
-    direct = (1, 3) if RELAY else (1, 3, 2)
+    direct = (1, 3)
 
     def forward(k):
         for h in direct:
@@ -183,13 +193,14 @@
                 ring_copy(h, k, True).start()
 
     def second(k):
-        ring_copy(1 if k % 2 == 0 else 3, k, False).wait_recv()
+        ring_copy(via(k), k, False).wait_recv()
         second_copy(k).start()
 
     def arrived(k):
-        for h in TILES:
-            if not (RELAY and h == (1 if k % 2 == 0 else 3)):
-                ring_copy(h, k, False).wait_recv()
+        for j in range(k * (FINE // CHUNKS), (k + 1) * (FINE // CHUNKS)):
+            for h in TILES:
+                if h != via(j):
+                    ring_copy(h, j, False).wait_recv()
 
     def column(h):
         tall = jnp.broadcast_to(labs[h][0:1, :].astype(jnp.float32), (half, half)).T
@@ -202,32 +213,63 @@
         for h in TILES:
             back_copy(h, k).start()
 
-    def stage(k):
-        arrived(k)
-        seq = split(unit_of(units[k].reshape((HOPS + 1) * rows, features))[0])
+    def weigh(raw, label):
+        seq = split(unit_of(raw)[0])
         st = (st_hi[...], st_lo[...])
         logit = scale * dot3(seq, st, ((1,), (1,))) + bias
-        label = columns[k].reshape((HOPS + 1) * rows, half)
         match = jnp.concatenate([label == label_rows[0], label == label_rows[1]], axis=1)
         margin = jnp.where(match, -logit, logit)
         small = jnp.exp(-jnp.abs(margin))
         loss = jnp.sum(jnp.maximum(margin, 0.0) + jnp.log1p(small), axis=1, keepdims=True)
-        loss = jnp.broadcast_to(loss, label.shape).reshape(HOPS + 1, rows, half)
-        columns[k] = loss
         sigmoid = jnp.where(margin >= 0.0, 1.0, small) / (1.0 + small)
         weight = split(jnp.where(match, -sigmoid, sigmoid))
-        parts[k] = dot3(weight, st, ((1,), (0,))).reshape(HOPS + 1, rows, features)
-        back(k)
-        towards = lax.dot_general(
+        return seq, weight, jnp.broadcast_to(loss, label.shape)
+
+    def towards(weight, seq):
+        return lax.dot_general(
             jnp.concatenate([weight[0], weight[1], weight[0]], axis=0),
             jnp.concatenate([seq[0], seq[0], seq[1]], axis=0),
             (((0,), (0,)), ((), ())),
             preferred_element_type=jnp.float32,
         )
-        if k == 0:
-            acc[...] = towards
+
+    def away(weight):
+        return dot3(weight, (st_hi[...], st_lo[...]), ((1,), (0,)))
+
+    def whole(h):
+        seq, weight, loss = weigh(
+            jnp.concatenate([units[k, h] for k in range(CHUNKS)], axis=0),
+            jnp.concatenate([columns[k, h] for k in range(CHUNKS)], axis=0),
+        )
+        result = away(weight)
+        for k in range(CHUNKS):
+            columns[k, h] = loss[k * rows : (k + 1) * rows]
+            parts[k, h] = result[k * rows : (k + 1) * rows]
+        if h == 0:
+            acc[...] = towards(weight, seq)
         else:
-            acc[...] += towards
+            acc[...] += towards(weight, seq)
+
+    visitors = pl.ds(1, RING - 1)
+
+    def stage(k):
+        arrived(k)
+        seq, weight, loss = weigh(
+            units[k, visitors].reshape((RING - 1) * rows, features), columns[k, visitors].reshape((RING - 1) * rows, half)
+        )
+        columns[k, visitors] = loss.reshape(RING - 1, rows, half)
+
+        def send_back():
+            parts[k, visitors] = away(weight).reshape(RING - 1, rows, features)
+            back(k)
+
+        if k < CHUNKS - 1:
+            send_back()
+        acc[...] += towards(weight, seq)
+        if k == CHUNKS - 1:
+            for p in range(PIECES):
+                acc_copy(p).start()
+            send_back()
 
     def collect(k):
         for h in TILES:
@@ -273,8 +315,9 @@
         def _():
             label_copy(h, False).start()
 
-    for k in range(CHUNKS):
+    for k in range(FINE):
         cross_copy(k).start()
+    for k in range(FINE):
         forward(k)
 
     column(0)
@@ -283,6 +326,7 @@
     st_hi[...], st_lo[...] = split(unit)
     for copy in load_seq:
         copy.wait()
+    whole(0)
     label_copy(HOPS, False).wait_recv()
     for h in TILES:
 
@@ -291,28 +335,29 @@
             label_copy(h, True).start()
 
     column(HOPS)
-    for k in range(CHUNKS):
+    for k in range(FINE):
         relay(k)
+        if k >= 4:
+            second(k - 4)
     for h in TILES:
         label_copy(h, False).wait_recv()
         column(h)
-    for k in range(READY if RELAY else 0):
+    for k in range(4, FINE):
+        if k == FOURTH + 2:
+            whole(HOPS)
         second(k)
     for k in range(CHUNKS):
         stage(k)
-        if RELAY and k + READY < CHUNKS:
-            second(k + READY)
-    for p in range(PIECES):
-        acc_copy(p).start()
-
-    for h in range(HOPS + 1):
-        tall = jnp.concatenate([columns[k, h] for k in range(CHUNKS)], axis=0)
-        losses[h] = tall.T[0:8, :]
-    for h in TILES:
-        loss_copy(h).start()
+
     for k in range(CHUNKS):
         collect(k)
-        if k == 1:
+        if k == 0:
+            for h in range(HOPS + 1):
+                tall = jnp.concatenate([columns[k, h] for k in range(CHUNKS)], axis=0)
+                losses[h] = tall.T[0:8, :]
+            for h in TILES:
+                loss_copy(h).start()
+        if k == 2:
             for h in TILES:
                 loss_copy(h).wait_recv()
             gone = losses[HOPS]
@@ -330,11 +375,13 @@
     loss_out[...] = (kept[0:1, :] + loss_cross[0:1, :]) / ((HOPS + 1) * 2.0 * half)
     put_loss.start()
 
+    for j in range(FINE):
+        cross_copy(j).wait_send()
+        for h in TILES:
+            ring_copy(h, j, False).wait_send()
     for k in range(CHUNKS):
-        cross_copy(k).wait_send()
         cross_back_copy(k).wait_send()
         for h in TILES:
-            ring_copy(h, k, False).wait_send()
             back_copy(h, k).wait_send()
     for h in TILES + (HOPS,):
         label_copy(h, False).wait_send()
@@ -401,10 +448,10 @@
             dma((1 + CHUNKS,)),
             dma((PIECES,)),
             dma((PIECES,)),
-            dma((CHUNKS,)),
-            dma((CHUNKS,)),
-            dma((RING - 1, CHUNKS)),
-            dma((RING - 1, CHUNKS)),
+            dma((FINE,)),
+            dma((FINE,)),
+            dma((RING - 1, FINE)),
+            dma((RING - 1, FINE)),
             dma((HOPS,)),
             dma((HOPS,)),
             dma((RING - 1, CHUNKS)),

time: 81 us -> 77.1 us (0.952)
  the two profiles are of different devices: /device:TPU:16 before, /device:TPU:1 now
where the time goes in v3:
time: 77.1 us; the launch traced here: 75.8 us
  Pallas kernels  73.9 us (96%)
  between operations  1.93 us (3%)
    pallas_call x1, Pallas kernels, body(): pl.pallas_call(functools.partial(kernel, groups), out_shape=(jax.ShapeDty...  71.6 us
    pallas_call x1, Pallas kernels, body(): pl.pallas_call(hand_over, out_shape=(jax.ShapeDtypeStruct((1, half), f32)...  2.25 us

profile of v3, /device:TPU:1, one launch (start us, length us, event | category | flops | bytes accessed | tf_op | source)
XLA Modules:
  0.0 75.8 jit_solution(12108975010672868564)
XLA Ops:
  1.9 71.6 %shard_map.76 = (f32[1,128]{1,0:T(1,128)}, f32[128,1024]{1,0:T(8,128)}, f32[256,1024]{1,0:T(8,128)}) custom-call(f32[128,1024]{1,0:T(8,128)} %seq_hbm.1, f32[256,1024]{1,0:T(8,128)} %st_hbm.1, s32[2,128]{1,0:T(2,128)} %bitcast.2, f32[1]{0:T(128)S(6)} %copy.8.scale_ref, f32[1]{0:T(128)S(6)} %copy.9.bias_ref), custom_call_target="tpu_custom_call" | custom-call | tf_op jit(solution)/shard_map/pallas_call | solution.py:418
  73.6 2.3 %hand_over.1 = (f32[1,128]{1,0:T(1,128)}, f32[128,1024]{1,0:T(8,128)}, f32[256,1024]{1,0:T(8,128)}) custom-call(f32[1,128]{1,0:T(1,128)} %get-tuple-element.9.a, f32[128,1024]{1,0:T(8,128)} %get-tuple-element.10.b, f32[256,1024]{1,0:T(8,128)} %get-tuple-element.11.c), custom_call_target="tpu_custom_call" | custom-call | tf_op jit(solution)/shard_map/hand_over/pallas_call | solution.py:470

commit v4 on v3

--- a/solution.py
+++ b/solution.py
@@ -263,13 +263,11 @@
             parts[k, visitors] = away(weight).reshape(RING - 1, rows, features)
             back(k)
 
-        if k < CHUNKS - 1:
-            send_back()
+        send_back()
         acc[...] += towards(weight, seq)
         if k == CHUNKS - 1:
             for p in range(PIECES):
                 acc_copy(p).start()
-            send_back()
 
     def collect(k):
         for h in TILES:
@@ -326,7 +324,6 @@
     st_hi[...], st_lo[...] = split(unit)
     for copy in load_seq:
         copy.wait()
-    whole(0)
     label_copy(HOPS, False).wait_recv()
     for h in TILES:
 
@@ -337,6 +334,8 @@
     column(HOPS)
     for k in range(FINE):
         relay(k)
+        if k == 1:
+            whole(0)
         if k >= 4:
             second(k - 4)
     for h in TILES:

time: 77.1 us -> 79.3 us (1.029)
  the two profiles are of different devices: /device:TPU:1 before, /device:TPU:2 now
where the time goes in v4:
time: 79.3 us; the launch traced here: 79.1 us
  Pallas kernels  77.2 us (97%)
  between operations  1.93 us (2%)
    pallas_call x1, Pallas kernels, body(): pl.pallas_call(functools.partial(kernel, groups), out_shape=(jax.ShapeDty...  75 us
    pallas_call x1, Pallas kernels, body(): pl.pallas_call(hand_over, out_shape=(jax.ShapeDtypeStruct((1, half), f32)...  2.25 us

profile of v4, /device:TPU:2, one launch (start us, length us, event | category | flops | bytes accessed | tf_op | source)
XLA Modules:
  0.0 79.1 jit_solution(16364730084281498531)
XLA Ops:
  1.9 75.0 %shard_map.76 = (f32[1,128]{1,0:T(1,128)}, f32[128,1024]{1,0:T(8,128)}, f32[256,1024]{1,0:T(8,128)}) custom-call(f32[128,1024]{1,0:T(8,128)} %seq_hbm.1, f32[256,1024]{1,0:T(8,128)} %st_hbm.1, s32[2,128]{1,0:T(2,128)} %bitcast.2, f32[1]{0:T(128)S(6)} %copy.8.scale_ref, f32[1]{0:T(128)S(6)} %copy.9.bias_ref), custom_call_target="tpu_custom_call" | custom-call | tf_op jit(solution)/shard_map/pallas_call | solution.py:417
  76.9 2.3 %hand_over.1 = (f32[1,128]{1,0:T(1,128)}, f32[128,1024]{1,0:T(8,128)}, f32[256,1024]{1,0:T(8,128)}) custom-call(f32[1,128]{1,0:T(1,128)} %get-tuple-element.9.a, f32[128,1024]{1,0:T(8,128)} %get-tuple-element.10.b, f32[256,1024]{1,0:T(8,128)} %get-tuple-element.11.c), custom_call_target="tpu_custom_call" | custom-call | tf_op jit(solution)/shard_map/hand_over/pallas_call | solution.py:469
